TPU v7x, 32 devices: a whole 2x2x4 slice. The times are simulated.
32 devices in a mesh: layer: 8 (over z, y), dp: 4 (over x, core).
Axes of the slice: x: 2, y: 2, z: 4, core: 2. Of those that a mesh axis runs over, the one named last changes fastest.
Arguments:
- states: float32 [8, 4, 256, 512], P('layer', 'dp'), may hold values from -6 to 6
- target: float32 [4, 256, 512], P('dp'), may hold values from -6 to 6
- lengths: int32 [4], P('dp'), may hold values from 64 to 256, as said below
- qkv_weight: bfloat16 [16, 512, 1536], P('layer'), may hold values from -0.25 to 0.25
- out_weight: bfloat16 [16, 512, 512], P('layer'), may hold values from -0.25 to 0.25
- up_weight: bfloat16 [16, 512, 1024], P('layer'), may hold values from -0.25 to 0.25
- down_weight: bfloat16 [16, 1024, 512], P('layer'), may hold values from -0.1875 to 0.1875
Outputs:
- block_ends: float32 [8, 4, 256, 512], P('layer', 'dp')
- adjoint_starts: float32 [8, 4, 256, 512], P('layer', 'dp')
- grad_qkv: float32 [16, 512, 1536], P('layer')
- grad_out: float32 [16, 512, 512], P('layer')
- grad_up: float32 [16, 512, 1024], P('layer')
- grad_down: float32 [16, 1024, 512], P('layer')
Inputs may be any that keep to these rules, and one draw needn't show every extreme that they name: A sequence's valid tokens are its first lengths entries; in every draw some sequence has all 256.
All inputs are finite; a program needn't handle non-finite values.
Results may differ from a plain program's by a relative error of at most 0.024.
Values sent between devices are 32-bit elements; how exact they have to be, the bound alone decides.
No kernel may reach another device: no remote copies, remote signals or barrier semaphores. Data moves between devices by JAX's collectives and lax.ppermute only.
A program may use at most 192 MiB of HBM per device.

v0:
```python
import math

import jax
import jax.numpy as jnp
from jax import lax
from jax.sharding import PartitionSpec as P

HEADS = 8


STEP = 0.125


def shifted(block, axis, distance):
    devices = range(lax.axis_size(axis))
    route = [(i - distance, i) for i in devices if i - distance in devices]
    return lax.ppermute(block, axis, route)


def layer_rows(inputs, weight_set, lengths):
    qkv_w, out_w, up_w, down_w = weight_set
    batch_size, row_count, model_width = inputs.shape
    head_dim = model_width // HEADS
    normed = (inputs * lax.rsqrt(jnp.mean(inputs * inputs, axis=-1, keepdims=True) + 1e-06)).astype(
        jnp.bfloat16
    )
    flat = normed.reshape(batch_size * row_count, model_width)
    packed = jnp.dot(flat, qkv_w, preferred_element_type=jnp.float32).astype(jnp.bfloat16)
    packed = packed.reshape(batch_size, row_count, 3, HEADS, head_dim)
    queries = packed[:, :, 0]
    new_keys = packed[:, :, 1]
    new_vals = packed[:, :, 2]
    scores = jnp.einsum(
        "bqhd,bkhd->bhqk", queries, new_keys, preferred_element_type=jnp.float32
    ) * head_dim ** (-0.5)
    query_pos = jnp.arange(row_count)
    key_pos = jnp.arange(new_keys.shape[1])
    causal = (key_pos[None, :] <= query_pos[:, None])[None, None]
    inside = (key_pos[None, :] < lengths[:, None])[:, None, None, :]
    scores = jnp.where(causal & inside, scores, -jnp.inf)
    attn_probs = jax.nn.softmax(scores, axis=-1).astype(jnp.bfloat16)
    context = jnp.einsum(
        "bhqk,bkhd->bqhd", attn_probs, new_vals, preferred_element_type=jnp.float32
    ).astype(jnp.bfloat16)
    context = context.reshape(batch_size * row_count, model_width)
    attn_out = jnp.dot(context, out_w, preferred_element_type=jnp.float32)
    hidden = jax.nn.gelu(jnp.dot(flat, up_w, preferred_element_type=jnp.float32)).astype(
        jnp.bfloat16
    )
    ffn_out = jnp.dot(hidden, down_w, preferred_element_type=jnp.float32)
    return ((attn_out + ffn_out).reshape(batch_size, row_count, model_width), new_keys, new_vals)


def on_device(states, target, lengths, qkv_weight, out_weight, up_weight, down_weight):
    layer_count = lax.axis_size("layer")
    device = lax.axis_index("layer")
    weight_list = (qkv_weight, out_weight, up_weight, down_weight)
    even_set = tuple((weight[0] for weight in weight_list))
    odd_set = tuple((weight[1] for weight in weight_list))
    starts = states[0]

    def apply_full(inputs, weight_set):
        return layer_rows(inputs, weight_set, lengths)[0]

    first_mid = starts + STEP * apply_full(starts, even_set)
    first_end = first_mid + STEP * apply_full(first_mid, odd_set)
    received = shifted(first_end, "layer", 1)
    relaxed = jnp.where(device == 0, starts, received)
    layer_out = apply_full(relaxed, even_set)
    fine_mid = relaxed + STEP * layer_out
    fine_end = fine_mid + STEP * apply_full(fine_mid, odd_set)
    defect = fine_end - (relaxed + 2.0 * STEP * layer_out)

    def active_whole(current):
        value = apply_full(current, even_set)
        return (current + STEP * value, current + 2.0 * STEP * value + defect)

    def round_whole(round_index, carry):
        current, middles, ends = carry
        middles, ends = lax.cond(
            device == round_index, lambda: active_whole(current), lambda: (middles, ends)
        )
        incoming = shifted(ends, "layer", 1)
        current = jnp.where(device == round_index + 1, incoming, current)
        return (current, middles, ends)

    corrected, middles, ends = lax.fori_loop(
        0, layer_count - 1, round_whole, (relaxed, jnp.zeros_like(relaxed), jnp.zeros_like(relaxed))
    )
    middles, ends = lax.cond(
        device == layer_count - 1, lambda: active_whole(corrected), lambda: (middles, ends)
    )
    valid = (jnp.arange(starts.shape[1])[None, :] < lengths[:, None]).astype(jnp.float32)[
        :, :, None
    ]
    guess = valid * (ends - target)

    def linearize(inputs, weight_set):
        _, pullback = jax.vjp(
            lambda moved, params: layer_rows(moved, params, lengths)[0], inputs, weight_set
        )
        return pullback

    odd_pull = linearize(middles, odd_set)
    even_pull = linearize(corrected, even_set)

    def odd_back(cotangent):
        return cotangent + STEP * odd_pull(cotangent)[0]

    def even_back(cotangent):
        return cotangent + STEP * even_pull(cotangent)[0]

    received_adj = shifted(even_back(odd_back(guess)), "layer", -1)
    relaxed_adj = jnp.where(device == layer_count - 1, guess, received_adj)
    fine_back = even_back(odd_back(relaxed_adj))

    def adjoint_value(current):
        gap = current - relaxed_adj
        return fine_back + (gap + 2.0 * STEP * even_pull(gap)[0])

    def round_adjoint(round_index, carry):
        current, kept = carry
        kept = lax.cond(
            device == layer_count - 1 - round_index, lambda: adjoint_value(current), lambda: kept
        )
        incoming = shifted(kept, "layer", -1)
        current = jnp.where(device == layer_count - 2 - round_index, incoming, current)
        return (current, kept)

    adjoint_ends, kept = lax.fori_loop(
        0, layer_count - 1, round_adjoint, (guess, jnp.zeros_like(guess))
    )
    adjoint_out = lax.cond(device == 0, lambda: adjoint_value(adjoint_ends), lambda: kept)
    odd_state, odd_grads = odd_pull(adjoint_ends)
    odd_final = adjoint_ends + STEP * odd_state
    even_grads = even_pull(odd_final)[1]
    partial_grads = tuple(
        (
            jnp.stack([STEP * even_g.astype(jnp.float32), STEP * odd_g.astype(jnp.float32)])
            for even_g, odd_g in zip(even_grads, odd_grads)
        )
    )
    count = float(sum((math.prod(weight.shape[1:]) for weight in weight_list)))
    totals = lax.psum(partial_grads, "dp")
    square = sum((jnp.sum(total * total, axis=(1, 2)) for total in totals))
    scale = jnp.sqrt(square / count + 1e-06)[:, None, None]
    results = tuple((total / scale for total in totals))
    return (ends[None], adjoint_out[None], results[0], results[1], results[2], results[3])


def solution(mesh):
    in_specs = (
        P("layer", "dp", None, None),
        P("dp", None, None),
        P("dp"),
        P("layer", None, None),
        P("layer", None, None),
        P("layer", None, None),
        P("layer", None, None),
    )
    out_specs = (
        P("layer", "dp", None, None),
        P("layer", "dp", None, None),
        P("layer", None, None),
        P("layer", None, None),
        P("layer", None, None),
        P("layer", None, None),
    )
    return jax.shard_map(
        on_device, mesh=mesh, in_specs=in_specs, out_specs=out_specs, check_vma=False
    )
```

profile of v0, /device:TPU:0, one launch (start us, length us, event | category | flops | bytes accessed | tf_op | source)
XLA Modules:
  0.0 893.4 jit_solution(2578411928533443741)
XLA Ops:
  14.0 3.3 multiply_reduce_fusion.11
  22.1 3.3 fusion.241
  25.3 5.2 collective-permute-start.2
  36.4 5.4 collective-permute-done.2
  48.2 2.5 multiply_reduce_fusion.9
  59.2 3.3 fusion.244
  63.3 128.6 %while.39 = (s32[]{:T(128)}, f32[1,256,512]{2,1,0:T(8,128)S(1)}, f32[1,256,512]{2,1,0:T(8,128)S(1)}, f32[1,256,512]{2,1,0:T(8,128)}, s32[]{:T(128)}, /*index=5*/...) while((s32[]{:T(128)}, f32[1,256,512]{2,1,0:T(8,128)S(1)}, ...), condition=%wide.region_18.19_spmd, body=%wide.region_12.18_spmd.sunk | while | flops 1284508672 | bytes 19617588 | solution.py:87
  63.4 10.6 %conditional.9 = ((f32[1,256,512]{2,1,0:T(8,128)S(1)}, f32[1,256,512]{2,1,0:T(8,128)})) conditional(s32[]{:T(128)} %convert_element_type.1480, (f32[1,256,512]{2,1,0:T(8,128)S(1)}, f32[1,256,512]{2,1,0:T(8,128)}) %tuple.172, (f32[1,256,512]{2,1,0:T(8,128)S(1)}, bf16[512,1536]{1,0:T(8,128)(2,1)S(1)}, s32[1]{0:T(128)}, bf16[512,512]{1,0:T(8,128)(2,1)}, ...), branch_computations={%region_13.13_spmd, %region_14.17_spmd} | conditional | flops 1284377600 | bytes 15947320 | solution.py:80
  70.5 3.4 fusion.16
  75.3 10.8 %collective-permute-done = f32[1,256,512]{2,1,0:T(8,128)S(1)} collective-permute-done((f32[1,256,512]{2,1,0:T(8,128)}, f32[1,256,512]{2,1,0:T(8,128)S(1)}, u32[]{:S(2)}, u32[]{:S(2)}) %collective-permute-start) | collective-permute-done | bytes 524320 | tf_op jit(solution)/shard_map/while/body/eval_jaxpr/ppermute | solution.py:17
  86.3 14.8 %collective-permute-start = (f32[1,256,512]{2,1,0:T(8,128)}, f32[1,256,512]{2,1,0:T(8,128)S(1)}, u32[]{:S(2)}, u32[]{:S(2)}) collective-permute-start(f32[1,256,512]{2,1,0:T(8,128)} %get-tuple-element.1386), channel_id=1, source_target_pairs={{0,4},{4,8},{8,12},{12,16},{16,20},{20,24},{24,28},{1,5},{5,9},{9,... | collective-permute-start | bytes 1572872 | tf_op jit(solution)/shard_map/while/body/eval_jaxpr/ppermute | solution.py:17
  101.1 9.9 %collective-permute-done = f32[1,256,512]{2,1,0:T(8,128)S(1)} collective-permute-done((f32[1,256,512]{2,1,0:T(8,128)}, f32[1,256,512]{2,1,0:T(8,128)S(1)}, u32[]{:S(2)}, u32[]{:S(2)}) %collective-permute-start) | collective-permute-done | bytes 524320 | tf_op jit(solution)/shard_map/while/body/eval_jaxpr/ppermute | solution.py:17
  111.2 4.3 collective-permute-start
  115.5 9.0 %collective-permute-done = f32[1,256,512]{2,1,0:T(8,128)S(1)} collective-permute-done((f32[1,256,512]{2,1,0:T(8,128)}, f32[1,256,512]{2,1,0:T(8,128)S(1)}, u32[]{:S(2)}, u32[]{:S(2)}) %collective-permute-start) | collective-permute-done | bytes 524320 | tf_op jit(solution)/shard_map/while/body/eval_jaxpr/ppermute | solution.py:17
  124.7 13.9 %collective-permute-start = (f32[1,256,512]{2,1,0:T(8,128)}, f32[1,256,512]{2,1,0:T(8,128)S(1)}, u32[]{:S(2)}, u32[]{:S(2)}) collective-permute-start(f32[1,256,512]{2,1,0:T(8,128)} %get-tuple-element.1386), channel_id=1, source_target_pairs={{0,4},{4,8},{8,12},{12,16},{16,20},{20,24},{24,28},{1,5},{5,9},{9,... | collective-permute-start | bytes 1572872 | tf_op jit(solution)/shard_map/while/body/eval_jaxpr/ppermute | solution.py:17
  138.7 8.4 collective-permute-done
  147.2 5.2 collective-permute-start
  152.4 7.4 collective-permute-done
  160.0 12.4 %collective-permute-start = (f32[1,256,512]{2,1,0:T(8,128)}, f32[1,256,512]{2,1,0:T(8,128)S(1)}, u32[]{:S(2)}, u32[]{:S(2)}) collective-permute-start(f32[1,256,512]{2,1,0:T(8,128)} %get-tuple-element.1386), channel_id=1, source_target_pairs={{0,4},{4,8},{8,12},{12,16},{16,20},{20,24},{24,28},{1,5},{5,9},{9,... | collective-permute-start | bytes 1572872 | tf_op jit(solution)/shard_map/while/body/eval_jaxpr/ppermute | solution.py:17
  172.5 7.0 collective-permute-done
  179.6 5.2 collective-permute-start
  184.8 7.0 collective-permute-done
  192.8 3.2 convolution_convert_fusion.23
  211.5 3.4 divide_convert_fusion.5
  217.7 3.8 convolution_convert_fusion.50
  234.4 2.6 multiply_multiply_fusion.13
  239.9 3.9 convolution_convert_fusion.49
  252.8 15.0 %collective-permute-done.3 = f32[1,256,512]{2,1,0:T(8,128)S(1)} collective-permute-done((f32[1,256,512]{2,1,0:T(8,128)S(1)}, f32[1,256,512]{2,1,0:T(8,128)S(1)}, u32[]{:S(2)}, u32[]{:S(2)}) %collective-permute-start.3) | collective-permute-done | bytes 524320 | tf_op jit(solution)/shard_map/ppermute | solution.py:17
  270.8 4.0 convolution_convert_fusion.48
  286.3 4.0 convolution_convert_fusion.47
  301.4 220.5 %while.40 = (s32[]{:T(128)}, f32[1,256,512]{2,1,0:T(8,128)S(1)}, f32[1,256,512]{2,1,0:T(8,128)}, s32[]{:T(128)}, f32[1,256,512]{2,1,0:T(8,128)}, /*index=5*/bf16...) while((s32[]{:T(128)}, f32[1,256,512]{2,1,0:T(8,128)S(1)}, ...), condition=%wide.region_44.45_spmd.clone, body=%wide.region_39.0_spmd.clone.sunk | while | flops 1356988672 | bytes 48437908 | solution.py:130
  302.7 11.2 %collective-permute-done.1 = f32[1,256,512]{2,1,0:T(8,128)S(1)} collective-permute-done((f32[1,256,512]{2,1,0:T(8,128)}, f32[1,256,512]{2,1,0:T(8,128)S(1)}, u32[]{:S(2)}, u32[]{:S(2)}) %collective-permute-start.1) | collective-permute-done | bytes 524320 | tf_op jit(solution)/shard_map/while/body/eval_jaxpr/ppermute | solution.py:17
  315.5 22.8 %collective-permute-done.1 = f32[1,256,512]{2,1,0:T(8,128)S(1)} collective-permute-done((f32[1,256,512]{2,1,0:T(8,128)}, f32[1,256,512]{2,1,0:T(8,128)S(1)}, u32[]{:S(2)}, u32[]{:S(2)}) %collective-permute-start.1) | collective-permute-done | bytes 524320 | tf_op jit(solution)/shard_map/while/body/eval_jaxpr/ppermute | solution.py:17
  339.8 10.0 %collective-permute-done.1 = f32[1,256,512]{2,1,0:T(8,128)S(1)} collective-permute-done((f32[1,256,512]{2,1,0:T(8,128)}, f32[1,256,512]{2,1,0:T(8,128)S(1)}, u32[]{:S(2)}, u32[]{:S(2)}) %collective-permute-start.1) | collective-permute-done | bytes 524320 | tf_op jit(solution)/shard_map/while/body/eval_jaxpr/ppermute | solution.py:17
  351.2 25.3 %collective-permute-done.1 = f32[1,256,512]{2,1,0:T(8,128)S(1)} collective-permute-done((f32[1,256,512]{2,1,0:T(8,128)}, f32[1,256,512]{2,1,0:T(8,128)S(1)}, u32[]{:S(2)}, u32[]{:S(2)}) %collective-permute-start.1) | collective-permute-done | bytes 524320 | tf_op jit(solution)/shard_map/while/body/eval_jaxpr/ppermute | solution.py:17
  378.0 15.9 %collective-permute-done.1 = f32[1,256,512]{2,1,0:T(8,128)S(1)} collective-permute-done((f32[1,256,512]{2,1,0:T(8,128)}, f32[1,256,512]{2,1,0:T(8,128)S(1)}, u32[]{:S(2)}, u32[]{:S(2)}) %collective-permute-start.1) | collective-permute-done | bytes 524320 | tf_op jit(solution)/shard_map/while/body/eval_jaxpr/ppermute | solution.py:17
  395.4 10.0 %collective-permute-done.1 = f32[1,256,512]{2,1,0:T(8,128)S(1)} collective-permute-done((f32[1,256,512]{2,1,0:T(8,128)}, f32[1,256,512]{2,1,0:T(8,128)S(1)}, u32[]{:S(2)}, u32[]{:S(2)}) %collective-permute-start.1) | collective-permute-done | bytes 524320 | tf_op jit(solution)/shard_map/while/body/eval_jaxpr/ppermute | solution.py:17
  406.9 114.7 %collective-permute-done.1 = f32[1,256,512]{2,1,0:T(8,128)S(1)} collective-permute-done((f32[1,256,512]{2,1,0:T(8,128)}, f32[1,256,512]{2,1,0:T(8,128)S(1)}, u32[]{:S(2)}, u32[]{:S(2)}) %collective-permute-start.1) | collective-permute-done | bytes 524320 | tf_op jit(solution)/shard_map/while/body/eval_jaxpr/ppermute | solution.py:17
  524.1 3.3 fusion.315
  557.7 4.3 multiply_bitcast_fusion.5
  567.2 2.6 pad_maximum_fusion.2
  574.4 3.4 pad_maximum_fusion
  578.9 19.1 %conditional.5 = (f32[1,1,256,512]{3,2,1,0:T(8,128)}) conditional(s32[]{:T(128)} %convert_element_type.750, f32[1,256,512]{2,1,0:T(8,128)} %get-tuple-element.836, (f32[1,256,512]{2,1,0:T(8,128)S(1)}, f32[1,256,512]{2,1,0:T(8,128)}, bf16[1024,512]{1,0:T(8,128)(2,1)}, f32[256,1024]{1,0:T(8,128)}, f32[256,1024]{1,0:T(8,128)}, ...), branch_computations={%region_45.46_spmd, %region_46.49_spmd} | conditional | flops 1356857600 | bytes 44767380 | solution.py:133
  580.8 5.5 convolution_convert_fusion.14
  598.0 269.6 %all-reduce.27.cloned.1.call-done = (f32[2,512,1536]{2,1,0:T(8,128)}, f32[2,1024,512]{2,1,0:T(8,128)}, f32[2,512,1024]{2,1,0:T(8,128)}, f32[2,512,512]{2,1,0:T(8,128)}) async-done(((f32[2,512,1536]{2,1,0:T(8,128)}, f32[2,1024,512]{2,1,0:T(8,128)}, f32[2,512,1024]{2,1,0:T(8,128)}, f32[2,512,512]{2,1,0:T(8,128)}), (f32[2,512,1536]{2,1,0:T(8,128)}, f32[2,1024,512]{2,1,0:T(8,128)}, f32[2,512,1024]{2,1,0:T(8,128)}, ...) | async-done | bytes 16777232 | tf_op jit(solution)/shard_map/psum | solution.py:144
  867.6 3.8 multiply_reduce_fusion.4
  875.7 2.7 broadcast_divide_fusion.1
  882.7 3.4 broadcast_divide_fusion
  (358 shorter events, 186.2 us)
Async XLA Ops:
  7.2 860.4 %all-reduce.27.cloned.1.call-start = ((), (), s32[]{:S(2)}) async-start(), calls=%async_computation | async-start | bytes 33554432 | tf_op jit(solution)/shard_map/psum | solution.py:144
  25.3 8.4 copy-start.39
  25.3 16.5 %collective-permute-start.2 = (f32[1,256,512]{2,1,0:T(8,128)}, f32[1,256,512]{2,1,0:T(8,128)S(1)}, u32[]{:S(2)}, u32[]{:S(2)}) collective-permute-start(f32[1,256,512]{2,1,0:T(8,128)} %fusion.241), channel_id=1, source_target_pairs={{0,4},{4,8},{8,12},{12,16},{16,20},{20,24},{24,28},{1,5},{5,9},{9,... | collective-permute-start | bytes 1572872 | tf_op jit(solution)/shard_map/ppermute | solution.py:17
  34.8 7.2 copy-start.50
  73.9 12.2 %collective-permute-start = (f32[1,256,512]{2,1,0:T(8,128)}, f32[1,256,512]{2,1,0:T(8,128)S(1)}, u32[]{:S(2)}, u32[]{:S(2)}) collective-permute-start(f32[1,256,512]{2,1,0:T(8,128)} %get-tuple-element.1386), channel_id=1, source_target_pairs={{0,4},{4,8},{8,12},{12,16},{16,20},{20,24},{24,28},{1,5},{5,9},{9,... | collective-permute-start | bytes 1572872 | tf_op jit(solution)/shard_map/while/body/eval_jaxpr/ppermute | solution.py:17
  86.3 24.8 %collective-permute-start = (f32[1,256,512]{2,1,0:T(8,128)}, f32[1,256,512]{2,1,0:T(8,128)S(1)}, u32[]{:S(2)}, u32[]{:S(2)}) collective-permute-start(f32[1,256,512]{2,1,0:T(8,128)} %get-tuple-element.1386), channel_id=1, source_target_pairs={{0,4},{4,8},{8,12},{12,16},{16,20},{20,24},{24,28},{1,5},{5,9},{9,... | collective-permute-start | bytes 1572872 | tf_op jit(solution)/shard_map/while/body/eval_jaxpr/ppermute | solution.py:17
  111.2 13.3 %collective-permute-start = (f32[1,256,512]{2,1,0:T(8,128)}, f32[1,256,512]{2,1,0:T(8,128)S(1)}, u32[]{:S(2)}, u32[]{:S(2)}) collective-permute-start(f32[1,256,512]{2,1,0:T(8,128)} %get-tuple-element.1386), channel_id=1, source_target_pairs={{0,4},{4,8},{8,12},{12,16},{16,20},{20,24},{24,28},{1,5},{5,9},{9,... | collective-permute-start | bytes 1572872 | tf_op jit(solution)/shard_map/while/body/eval_jaxpr/ppermute | solution.py:17
  124.7 22.3 %collective-permute-start = (f32[1,256,512]{2,1,0:T(8,128)}, f32[1,256,512]{2,1,0:T(8,128)S(1)}, u32[]{:S(2)}, u32[]{:S(2)}) collective-permute-start(f32[1,256,512]{2,1,0:T(8,128)} %get-tuple-element.1386), channel_id=1, source_target_pairs={{0,4},{4,8},{8,12},{12,16},{16,20},{20,24},{24,28},{1,5},{5,9},{9,... | collective-permute-start | bytes 1572872 | tf_op jit(solution)/shard_map/while/body/eval_jaxpr/ppermute | solution.py:17
  147.2 12.7 %collective-permute-start = (f32[1,256,512]{2,1,0:T(8,128)}, f32[1,256,512]{2,1,0:T(8,128)S(1)}, u32[]{:S(2)}, u32[]{:S(2)}) collective-permute-start(f32[1,256,512]{2,1,0:T(8,128)} %get-tuple-element.1386), channel_id=1, source_target_pairs={{0,4},{4,8},{8,12},{12,16},{16,20},{20,24},{24,28},{1,5},{5,9},{9,... | collective-permute-start | bytes 1572872 | tf_op jit(solution)/shard_map/while/body/eval_jaxpr/ppermute | solution.py:17
  160.0 19.4 %collective-permute-start = (f32[1,256,512]{2,1,0:T(8,128)}, f32[1,256,512]{2,1,0:T(8,128)S(1)}, u32[]{:S(2)}, u32[]{:S(2)}) collective-permute-start(f32[1,256,512]{2,1,0:T(8,128)} %get-tuple-element.1386), channel_id=1, source_target_pairs={{0,4},{4,8},{8,12},{12,16},{16,20},{20,24},{24,28},{1,5},{5,9},{9,... | collective-permute-start | bytes 1572872 | tf_op jit(solution)/shard_map/while/body/eval_jaxpr/ppermute | solution.py:17
  179.6 12.2 %collective-permute-start = (f32[1,256,512]{2,1,0:T(8,128)}, f32[1,256,512]{2,1,0:T(8,128)S(1)}, u32[]{:S(2)}, u32[]{:S(2)}) collective-permute-start(f32[1,256,512]{2,1,0:T(8,128)} %get-tuple-element.1386), channel_id=1, source_target_pairs={{0,4},{4,8},{8,12},{12,16},{16,20},{20,24},{24,28},{1,5},{5,9},{9,... | collective-permute-start | bytes 1572872 | tf_op jit(solution)/shard_map/while/body/eval_jaxpr/ppermute | solution.py:17
  192.7 4.8 copy-start.17
  192.7 3.4 copy-start.40
  192.8 4.7 copy-start.43
  198.3 2.9 copy-start.55
  201.2 3.2 copy-start.31
  209.4 6.9 copy-start.45
  211.5 3.4 copy-start.25
  217.7 3.8 copy-start.66
  221.6 2.8 copy-start.18
  221.6 2.9 copy-start.84
  224.4 3.2 copy-start.10
  231.3 5.6 copy-start.6
  244.9 3.9 copy-start.20
  247.2 3.6 copy-start.7
  247.4 21.3 %copy-start.11 = (bf16[2,512,512]{2,1,0:T(8,128)(2,1)S(1)}, bf16[2,512,512]{2,1,0:T(8,128)(2,1)}, u32[]{:S(2)}) copy-start(bf16[2,512,512]{2,1,0:T(8,128)(2,1)} %param.23) | copy-start | bytes 3145732
  247.4 20.4 %collective-permute-start.3 = (f32[1,256,512]{2,1,0:T(8,128)S(1)}, f32[1,256,512]{2,1,0:T(8,128)S(1)}, u32[]{:S(2)}, u32[]{:S(2)}) collective-permute-start(f32[1,256,512]{2,1,0:T(8,128)S(1)} %fusion.451), channel_id=1, source_target_pairs={{4,0},{8,4},{12,8},{16,12},{20,16},{24,20},{28,24},{5,1},{9,5},{13... | collective-permute-start | bytes 1572872 | tf_op jit(solution)/shard_map/ppermute | solution.py:17
  282.5 2.7 copy-start.12
  290.3 3.6 copy-start.33
  301.4 12.5 %collective-permute-start.1 = (f32[1,256,512]{2,1,0:T(8,128)}, f32[1,256,512]{2,1,0:T(8,128)S(1)}, u32[]{:S(2)}, u32[]{:S(2)}) collective-permute-start(f32[1,256,512]{2,1,0:T(8,128)} %get-tuple-element.1492), channel_id=1, source_target_pairs={{4,0},{8,4},{12,8},{16,12},{20,16},{24,20},{28,24},{5,1},{9,5},{13... | collective-permute-start | bytes 1572872 | tf_op jit(solution)/shard_map/while/body/eval_jaxpr/ppermute | solution.py:17
  314.2 24.1 %collective-permute-start.1 = (f32[1,256,512]{2,1,0:T(8,128)}, f32[1,256,512]{2,1,0:T(8,128)S(1)}, u32[]{:S(2)}, u32[]{:S(2)}) collective-permute-start(f32[1,256,512]{2,1,0:T(8,128)} %get-tuple-element.1492), channel_id=1, source_target_pairs={{4,0},{8,4},{12,8},{16,12},{20,16},{24,20},{28,24},{5,1},{9,5},{13... | collective-permute-start | bytes 1572872 | tf_op jit(solution)/shard_map/while/body/eval_jaxpr/ppermute | solution.py:17
  338.5 11.3 %collective-permute-start.1 = (f32[1,256,512]{2,1,0:T(8,128)}, f32[1,256,512]{2,1,0:T(8,128)S(1)}, u32[]{:S(2)}, u32[]{:S(2)}) collective-permute-start(f32[1,256,512]{2,1,0:T(8,128)} %get-tuple-element.1492), channel_id=1, source_target_pairs={{4,0},{8,4},{12,8},{16,12},{20,16},{24,20},{28,24},{5,1},{9,5},{13... | collective-permute-start | bytes 1572872 | tf_op jit(solution)/shard_map/while/body/eval_jaxpr/ppermute | solution.py:17
  349.9 26.6 %collective-permute-start.1 = (f32[1,256,512]{2,1,0:T(8,128)}, f32[1,256,512]{2,1,0:T(8,128)S(1)}, u32[]{:S(2)}, u32[]{:S(2)}) collective-permute-start(f32[1,256,512]{2,1,0:T(8,128)} %get-tuple-element.1492), channel_id=1, source_target_pairs={{4,0},{8,4},{12,8},{16,12},{20,16},{24,20},{28,24},{5,1},{9,5},{13... | collective-permute-start | bytes 1572872 | tf_op jit(solution)/shard_map/while/body/eval_jaxpr/ppermute | solution.py:17
  376.7 17.2 %collective-permute-start.1 = (f32[1,256,512]{2,1,0:T(8,128)}, f32[1,256,512]{2,1,0:T(8,128)S(1)}, u32[]{:S(2)}, u32[]{:S(2)}) collective-permute-start(f32[1,256,512]{2,1,0:T(8,128)} %get-tuple-element.1492), channel_id=1, source_target_pairs={{4,0},{8,4},{12,8},{16,12},{20,16},{24,20},{28,24},{5,1},{9,5},{13... | collective-permute-start | bytes 1572872 | tf_op jit(solution)/shard_map/while/body/eval_jaxpr/ppermute | solution.py:17
  394.1 11.3 %collective-permute-start.1 = (f32[1,256,512]{2,1,0:T(8,128)}, f32[1,256,512]{2,1,0:T(8,128)S(1)}, u32[]{:S(2)}, u32[]{:S(2)}) collective-permute-start(f32[1,256,512]{2,1,0:T(8,128)} %get-tuple-element.1492), channel_id=1, source_target_pairs={{4,0},{8,4},{12,8},{16,12},{20,16},{24,20},{28,24},{5,1},{9,5},{13... | collective-permute-start | bytes 1572872 | tf_op jit(solution)/shard_map/while/body/eval_jaxpr/ppermute | solution.py:17
  405.6 116.0 %collective-permute-start.1 = (f32[1,256,512]{2,1,0:T(8,128)}, f32[1,256,512]{2,1,0:T(8,128)S(1)}, u32[]{:S(2)}, u32[]{:S(2)}) collective-permute-start(f32[1,256,512]{2,1,0:T(8,128)} %get-tuple-element.1492), channel_id=1, source_target_pairs={{4,0},{8,4},{12,8},{16,12},{20,16},{24,20},{28,24},{5,1},{9,5},{13... | collective-permute-start | bytes 1572872 | tf_op jit(solution)/shard_map/while/body/eval_jaxpr/ppermute | solution.py:17
  527.3 3.6 copy-start.47
  537.8 2.7 copy-start.48
  540.3 6.2 copy-start.34
  557.7 4.3 copy-start.64
  557.7 4.6 copy-start.67
  564.3 3.0 copy-start.61
  567.2 3.7 copy-start.60
  571.0 3.4 copy-start.24
  580.8 5.5 copy-start.28
  867.6 4.0 copy-start.22
  875.7 6.9 slice-start
  878.5 4.2 slice-start.1
  (50 other events, 90.7 us)
Sparse Core Ops, SparseCore 0:
  577.9 289.5 all-reduce.26
where the time goes:
time: 901 us; the launch traced here: 893 us
  waiting for transfers between devices  559 us (62%)
  matrix products  158 us (18%)
  starting transfers between devices  73 us (8%)
  local copies, waits for them, and re-layouts  44.1 us (5%)
  other arithmetic  40.9 us (5%)
  between operations  16.1 us (2%)
    ppermute x16, waiting for transfers between devices, shifted(): return lax.ppermute(block, axis, route)  290 us
    psum x1, waiting for transfers between devices, on_device(): totals = lax.psum(partial_grads, 'dp')  270 us
    ppermute x16, starting transfers between devices, shifted(): return lax.ppermute(block, axis, route)  72.9 us
    dot_general x21, matrix products, layer_rows(): jnp.einsum('bhqk,bkhd->bqhd', attn_probs, new_vals, preferred_element_typ...  39.2 us
    dot_general x10, matrix products, layer_rows(): jnp.dot(flat, up_w, preferred_element_type=jnp.float32)  31.7 us
    dot_general x15, matrix products, layer_rows(): jnp.dot(flat, qkv_w, preferred_element_type=jnp.float32)  23.4 us
    dot_general x8, matrix products, layer_rows(): ffn_out = jnp.dot(hidden, down_w, preferred_element_type=jnp.float32)  23 us
  transfers between devices with their start and end apart: 17, of which 17 were waited for; matrix products, arithmetic and copies ran while one was open for 3% of the time, Pallas kernels for 0%

commit v1 on v0

--- a/solution.py
+++ b/solution.py
@@ -65,44 +65,38 @@
     first_mid = starts + STEP * apply_full(starts, even_set)
     first_end = first_mid + STEP * apply_full(first_mid, odd_set)
     received = shifted(first_end, "layer", 1)
-    relaxed = jnp.where(device == 0, starts, received)
-    layer_out = apply_full(relaxed, even_set)
-    fine_mid = relaxed + STEP * layer_out
-    fine_end = fine_mid + STEP * apply_full(fine_mid, odd_set)
-    defect = fine_end - (relaxed + 2.0 * STEP * layer_out)
+    corrected = jnp.where(device == 0, starts, received)
+    layer_out = apply_full(corrected, even_set)
+    middles = corrected + STEP * layer_out
+    ends = middles + STEP * apply_full(middles, odd_set)
+    defect = ends - (corrected + 2.0 * STEP * layer_out)
 
     def active_whole(current):
         value = apply_full(current, even_set)
-        return (current + STEP * value, current + 2.0 * STEP * value + defect)
+        return (current, current + STEP * value, current + 2.0 * STEP * value + defect)
 
-    def round_whole(round_index, carry):
-        current, middles, ends = carry
-        middles, ends = lax.cond(
-            device == round_index, lambda: active_whole(current), lambda: (middles, ends)
+    for block in range(2, layer_count):
+        incoming = lax.ppermute(ends, "layer", [(block - 1, block)])
+        corrected, middles, ends = lax.cond(
+            device == block,
+            lambda: active_whole(incoming),
+            lambda: (corrected, middles, ends),
         )
-        incoming = shifted(ends, "layer", 1)
-        current = jnp.where(device == round_index + 1, incoming, current)
-        return (current, middles, ends)
-
-    corrected, middles, ends = lax.fori_loop(
-        0, layer_count - 1, round_whole, (relaxed, jnp.zeros_like(relaxed), jnp.zeros_like(relaxed))
-    )
-    middles, ends = lax.cond(
-        device == layer_count - 1, lambda: active_whole(corrected), lambda: (middles, ends)
-    )
+    all_lengths = lax.all_gather(lengths, "dp", tiled=True)
+    all_corrected = lax.all_gather(corrected, "dp", tiled=True)
     valid = (jnp.arange(starts.shape[1])[None, :] < lengths[:, None]).astype(jnp.float32)[
         :, :, None
     ]
     guess = valid * (ends - target)
 
-    def linearize(inputs, weight_set):
+    def linearize(inputs, weight_set, sizes):
         _, pullback = jax.vjp(
-            lambda moved, params: layer_rows(moved, params, lengths)[0], inputs, weight_set
+            lambda moved, params: layer_rows(moved, params, sizes)[0], inputs, weight_set
         )
         return pullback
 
-    odd_pull = linearize(middles, odd_set)
-    even_pull = linearize(corrected, even_set)
+    odd_pull = linearize(middles, odd_set, lengths)
+    even_pull = linearize(corrected, even_set, lengths)
 
     def odd_back(cotangent):
         return cotangent + STEP * odd_pull(cotangent)[0]
@@ -113,35 +107,31 @@
     received_adj = shifted(even_back(odd_back(guess)), "layer", -1)
     relaxed_adj = jnp.where(device == layer_count - 1, guess, received_adj)
     fine_back = even_back(odd_back(relaxed_adj))
+    adjoint_ends, adjoint_out = relaxed_adj, fine_back
 
     def adjoint_value(current):
         gap = current - relaxed_adj
-        return fine_back + (gap + 2.0 * STEP * even_pull(gap)[0])
+        return (current, fine_back + (gap + 2.0 * STEP * even_pull(gap)[0]))
 
-    def round_adjoint(round_index, carry):
-        current, kept = carry
-        kept = lax.cond(
-            device == layer_count - 1 - round_index, lambda: adjoint_value(current), lambda: kept
+    for block in range(layer_count - 3, -1, -1):
+        incoming = lax.ppermute(adjoint_out, "layer", [(block + 1, block)])
+        adjoint_ends, adjoint_out = lax.cond(
+            device == block,
+            lambda: adjoint_value(incoming),
+            lambda: (adjoint_ends, adjoint_out),
         )
-        incoming = shifted(kept, "layer", -1)
-        current = jnp.where(device == layer_count - 2 - round_index, incoming, current)
-        return (current, kept)
-
-    adjoint_ends, kept = lax.fori_loop(
-        0, layer_count - 1, round_adjoint, (guess, jnp.zeros_like(guess))
-    )
-    adjoint_out = lax.cond(device == 0, lambda: adjoint_value(adjoint_ends), lambda: kept)
-    odd_state, odd_grads = odd_pull(adjoint_ends)
-    odd_final = adjoint_ends + STEP * odd_state
-    even_grads = even_pull(odd_final)[1]
-    partial_grads = tuple(
+    all_adjoint = lax.all_gather(adjoint_ends, "dp", tiled=True)
+    all_middles = all_corrected + STEP * layer_rows(all_corrected, even_set, all_lengths)[0]
+    odd_state, odd_grads = linearize(all_middles, odd_set, all_lengths)(all_adjoint)
+    odd_final = all_adjoint + STEP * odd_state
+    even_grads = linearize(all_corrected, even_set, all_lengths)(odd_final)[1]
+    totals = tuple(
         (
             jnp.stack([STEP * even_g.astype(jnp.float32), STEP * odd_g.astype(jnp.float32)])
             for even_g, odd_g in zip(even_grads, odd_grads)
         )
     )
     count = float(sum((math.prod(weight.shape[1:]) for weight in weight_list)))
-    totals = lax.psum(partial_grads, "dp")
     square = sum((jnp.sum(total * total, axis=(1, 2)) for total in totals))
     scale = jnp.sqrt(square / count + 1e-06)[:, None, None]
     results = tuple((total / scale for total in totals))

time: 901 us -> 746 us (0.83)
  the two profiles are of different devices: /device:TPU:0 before, /device:TPU:4 now
where the time goes in v1:
time: 746 us; the launch traced here: 738 us
  waiting for transfers between devices  288 us (39%)
  matrix products  231 us (31%)
  local copies, waits for them, and re-layouts  109 us (15%)
  other arithmetic  50.1 us (7%)
  starting transfers between devices  25.7 us (3%)
  between operations  16.4 us (2%)
  loops' own time  13.1 us (2%)
    ppermute x6, waiting for transfers between devices, on_device(): incoming = lax.ppermute(adjoint_out, 'layer', [(block + 1, block)])  236 us
    dot_general x16, matrix products, layer_rows(): jnp.einsum('bqhd,bkhd->bhqk', queries, new_keys, preferred_element_type=j...  55.1 us
    dot_general x20, matrix products, layer_rows(): jnp.einsum('bhqk,bkhd->bqhd', attn_probs, new_vals, preferred_element_typ...  48.1 us
    dot_general x12, matrix products, layer_rows(): jnp.dot(flat, up_w, preferred_element_type=jnp.float32)  43.1 us
    ppermute x2, waiting for transfers between devices, shifted(): return lax.ppermute(block, axis, route)  42.9 us
    unnamed x185, local copies, waits for them, and re-layouts  41 us
    dot_general x16, matrix products, layer_rows(): jnp.dot(flat, qkv_w, preferred_element_type=jnp.float32)  32.1 us
    dot_general x8, matrix products, layer_rows(): ffn_out = jnp.dot(hidden, down_w, preferred_element_type=jnp.float32)  24.8 us
  transfers between devices with their start and end apart: 16, of which 4 were waited for; matrix products, arithmetic and copies ran while one was open for 20% of the time, Pallas kernels for 0%

profile of v1, /device:TPU:4, one launch (start us, length us, event | category | flops | bytes accessed | tf_op | source)
XLA Modules:
  0.0 737.7 jit_solution(500927337945093206)
XLA Ops:
  26.7 3.6 collective-permute-start
  35.1 7.2 collective-permute-done
  49.3 3.3 multiply_reduce_fusion.15
  62.2 3.6 fusion.876
  65.8 4.3 collective-permute-start.1
  71.7 9.1 %collective-permute-done.1 = f32[1,256,512]{2,1,0:T(8,128)S(1)} collective-permute-done((f32[1,256,512]{2,1,0:T(8,128)}, f32[1,256,512]{2,1,0:T(8,128)S(1)}, u32[]{:S(2)}, u32[]{:S(2)}) %collective-permute-start.1) | collective-permute-done | bytes 524320 | tf_op jit(solution)/shard_map/ppermute | solution.py:79
  89.7 7.0 conditional.17
  96.8 3.1 fusion.775
  105.0 3.2 fusion.1181
  112.5 3.5 divide_convert_fusion.15
  118.8 4.0 convolution_convert_fusion.98
  135.0 3.2 fusion.1182
  140.5 3.5 divide_convert_fusion.14
  149.9 3.8 convolution_convert_fusion.97
  161.6 35.8 %collective-permute-done.7 = f32[1,256,512]{2,1,0:T(8,128)S(1)} collective-permute-done((f32[1,256,512]{2,1,0:T(8,128)}, f32[1,256,512]{2,1,0:T(8,128)S(1)}, u32[]{:S(2)}, u32[]{:S(2)}) %collective-permute-start.7) | collective-permute-done | bytes 524320 | tf_op jit(solution)/shard_map/ppermute | solution.py:17
  197.4 3.8 convolution_convert_fusion.96
  210.2 4.0 convolution_convert_fusion.95
  230.8 3.1 conditional.18
  236.9 3.6 conditional.20
  243.4 4.9 all-reduce.36
  250.6 235.8 %collective-permute-done.12 = f32[1,256,512]{2,1,0:T(8,128)S(1)} collective-permute-done((f32[1,256,512]{2,1,0:T(8,128)}, f32[1,256,512]{2,1,0:T(8,128)S(1)}, u32[]{:S(2)}, u32[]{:S(2)}) %collective-permute-start.12) | collective-permute-done | bytes 524320 | tf_op jit(solution)/shard_map/ppermute | solution.py:117
  486.4 22.4 %conditional.22 = ((f32[1,256,512]{2,1,0:T(8,128)}, f32[1,256,512]{2,1,0:T(8,128)})) conditional(s32[]{:T(128)} %convert_element_type.1102, (f32[1,256,512]{2,1,0:T(8,128)}, f32[1,256,512]{2,1,0:T(8,128)}) %get-tuple-element.1274, (f32[1,256,512]{2,1,0:T(8,128)S(1)}, f32[1,256,512]{2,1,0:T(8,128)S(1)}, bf16[1024,512]{1,0:T(8,128)(2,1)}, ...), branch_computations={%region_73.74_spmd, %region_74.77_spmd} | conditional | flops 1356857600 | bytes 41490624 | solution.py:118
  488.3 4.6 convolution_convert_fusion.46
  516.7 3.5 convolution_convert_fusion.61
  523.0 9.2 %reshape.2113 = bf16[4,256,3,8,64]{4,3,2,1,0:T(8,128)(2,1)} reshape(bf16[1024,1536]{1,0:T(8,128)(2,1)} %convolution_convert_fusion.61) | data formatting | bytes 6291456 | tf_op jit(solution)/shard_map/reshape | solution.py:29
  532.2 5.7 fusion.1168
  537.9 3.0 copy.339
  541.0 3.0 copy.338
  547.0 6.1 fusion.759
  553.1 9.0 %fusion.1187 = (f32[4,8,256]{2,1,0:T(8,128)S(1)}, f32[4,8,256,256]{2,3,1,0:T(8,128)S(1)}) fusion(f32[4,8,256,256]{2,3,1,0:T(8,128)} %fusion.759, pred[4,256,256]{1,2,0:T(8,128)(4,1)S(1)} %copy-done.104), kind=kOutput, calls=%fused_computation.1372 | output fusion | flops 12583167 | bytes 17072128 | tf_op jit(solution)/shard_map/sub | solution.py:41
  577.3 5.8 reshape.2114
  583.1 5.3 fusion.1167
  590.6 3.1 copy.340
  598.2 4.5 fusion.1188
  603.3 3.3 fusion.771
  613.0 5.4 divide_convert_fusion.12
  618.4 7.1 fusion.639
  625.6 5.7 fusion.638
  637.1 3.6 multiply_bitcast_fusion
  644.2 3.7 fusion.535
  658.9 7.5 %fusion.530 = (f32[4,8,256]{2,1,0:T(8,128)S(1)}, bf16[4,8,256,256]{2,3,1,0:T(8,128)(2,1)}) fusion(f32[4,8,256,256]{2,3,1,0:T(8,128)} %copy-done.4, f32[4,8,256]{2,1,0:T(8,128)S(1)} %multiply_divide_fusion, bf16[4,256,1,8,64]{1,4,3,0,2:T(8,128)(2,1)S(1)} %copy-done.16, bf16[4,8,64,256]{3,0,2,1:T(4,128)(2,1)} %bitcast.1765), kind=kOutput, calls=%fused_computation.656 | convolution fusion | flops 278913024 | bytes 14745600 | tf_op jit(solution)/shard_map/transpose(jvp(bhqk,bkhd->bqhd))/dot_general | solution.py:42
  666.4 8.0 %fusion.641 = bf16[4,256,1,8,64]{1,4,3,0,2:T(8,128)(2,1)} fusion(bf16[4,256,1,8,64]{1,4,3,0,2:T(8,128)(2,1)S(1)} %copy-done.41, f32[4,8,256,256]{2,3,1,0:T(8,128)} %copy-done.4, bf16[4,8,256,256]{2,3,1,0:T(8,128)(2,1)} %get-tuple-element.1198, f32[4,8,256]{2,1,0:T(8,128)S(1)} %neg.87, f32[4,8,256]{2,1,0:T(8,128)S(1)} %get-tuple-element.1192, ...), kind=kOutput, calls=%fused_computation.862 | convolution fusion | flops 281542656 | bytes 15007744 | tf_op jit(solution)/shard_map/transpose(jvp(bqhd,bkhd->bhqk))/dot_general | solution.py:33
  674.5 6.0 fusion.640
  682.8 3.1 multiply_bitcast_fusion.2
  686.0 3.0 multiply_bitcast_fusion.3
  691.6 8.7 %multiply_bitcast_fusion.5 = f32[1,512,1024]{2,1,0:T(8,128)} fusion(bf16[1024,512]{1,0:T(8,128)(2,1)} %bitcast.1822, f32[1024,1024]{1,0:T(8,128)} %copy-done.118, bf16[1024,512]{1,0:T(8,128)(2,1)} %bitcast.1829, bf16[2,1024,512]{2,1,0:T(8,128)(2,1)} %param.37), kind=kOutput, calls=%fused_computation.775 | convolution fusion | flops 2170552320 | bytes 9437184 | tf_op jit(solution)/shard_map/transpose(jvp())/dot_general | solution.py:47
  700.3 3.2 fusion.637
  720.3 3.4 fusion.533
  (390 shorter events, 236.0 us)
Async XLA Ops:
  7.2 503.7 %all-gather.3.cloned.1.call-start = ((), (), s32[]{:S(2)}) async-start(), calls=%async_computation | async-start | bytes 2621440 | tf_op jit(solution)/shard_map/all_gather | solution.py:86
  26.7 15.6 %collective-permute-start = (f32[1,256,512]{2,1,0:T(8,128)S(1)}, f32[1,256,512]{2,1,0:T(8,128)S(1)}, u32[]{:S(2)}, u32[]{:S(2)}) collective-permute-start(f32[1,256,512]{2,1,0:T(8,128)S(1)} %fusion.654), channel_id=1, source_target_pairs={{0,4},{4,8},{8,12},{12,16},{16,20},{20,24},{24,28},{1,5},{5,9},{9,... | collective-permute-start | bytes 1572872 | tf_op jit(solution)/shard_map/ppermute | solution.py:17
  32.7 9.8 %copy-start.82 = (bf16[2,512,1536]{2,1,0:T(8,128)(2,1)S(1)}, bf16[2,512,1536]{2,1,0:T(8,128)(2,1)}, u32[]{:S(2)}) copy-start(bf16[2,512,1536]{2,1,0:T(8,128)(2,1)} %param.34) | copy-start | bytes 9437188
  65.8 14.9 %collective-permute-start.1 = (f32[1,256,512]{2,1,0:T(8,128)}, f32[1,256,512]{2,1,0:T(8,128)S(1)}, u32[]{:S(2)}, u32[]{:S(2)}) collective-permute-start(f32[1,256,512]{2,1,0:T(8,128)} %get-tuple-element.1172), channel_id=1, source_target_pairs={{4,8},{5,9},{6,10},{7,11}} | collective-permute-start | bytes 1572872 | tf_op jit(solution)/shard_map/ppermute | solution.py:79
  80.7 1.4 collective-permute-start.2
  82.4 1.5 collective-permute-start.3
  83.9 1.5 collective-permute-start.4
  85.3 1.5 collective-permute-start.5
  88.2 1.5 collective-permute-start.6
  96.7 31.3 %copy-start.18 = (f32[1,256,512]{2,1,0:T(8,128)}, f32[1,256,512]{2,1,0:T(8,128)S(1)}, u32[]{:S(2)}) copy-start(f32[1,256,512]{2,1,0:T(8,128)S(1)} %get-tuple-element.688) | copy-start | bytes 1572868
  96.7 61.8 %copy-start = (f32[1,256,512]{2,1,0:T(8,128)}, f32[1,256,512]{2,1,0:T(8,128)S(1)}, u32[]{:S(2)}) copy-start(f32[1,256,512]{2,1,0:T(8,128)S(1)} %get-tuple-element.690) | copy-start | bytes 1572868
  112.5 3.5 copy-start.59
  112.5 3.5 copy-start.65
  118.8 4.0 copy-start.75
  135.0 3.2 copy-start.38
  140.5 3.5 copy-start.39
  149.9 3.8 copy-start.76
  159.6 37.8 %collective-permute-start.7 = (f32[1,256,512]{2,1,0:T(8,128)}, f32[1,256,512]{2,1,0:T(8,128)S(1)}, u32[]{:S(2)}, u32[]{:S(2)}) collective-permute-start(f32[1,256,512]{2,1,0:T(8,128)} %fusion.853), channel_id=1, source_target_pairs={{4,0},{8,4},{12,8},{16,12},{20,16},{24,20},{28,24},{5,1},{9,5},{13... | collective-permute-start | bytes 1572872 | tf_op jit(solution)/shard_map/ppermute | solution.py:17
  161.5 445.0 %all-gather.5.cloned.1.call-start = ((), (), s32[]{:S(2)}) async-start(), calls=%async_computation.1 | async-start | bytes 2621440 | tf_op jit(solution)/shard_map/all_gather | solution.py:123
  210.2 4.0 copy-start.32
  222.0 4.3 copy-start.87
  228.3 1.6 collective-permute-start.8
  233.9 1.5 collective-permute-start.9
  235.4 1.5 collective-permute-start.10
  236.9 5.1 copy-start.122
  240.5 7.7 %collective-permute-start.11 = (f32[1,256,512]{2,1,0:T(8,128)}, f32[1,256,512]{2,1,0:T(8,128)}, u32[]{:S(2)}, u32[]{:S(2)}) collective-permute-start(f32[1,256,512]{2,1,0:T(8,128)} %get-tuple-element.694), channel_id=1, source_target_pairs={{12,8},{13,9},{14,10},{15,11}} | collective-permute-start | bytes 1572872 | tf_op jit(solution)/shard_map/ppermute | solution.py:117
  248.3 238.1 %collective-permute-start.12 = (f32[1,256,512]{2,1,0:T(8,128)}, f32[1,256,512]{2,1,0:T(8,128)S(1)}, u32[]{:S(2)}, u32[]{:S(2)}) collective-permute-start(f32[1,256,512]{2,1,0:T(8,128)} %get-tuple-element.695), channel_id=1, source_target_pairs={{8,4},{9,5},{10,6},{11,7}} | collective-permute-start | bytes 1572872 | tf_op jit(solution)/shard_map/ppermute | solution.py:117
  508.8 63.5 %collective-permute-start.13 = (f32[1,256,512]{2,1,0:T(8,128)}, f32[1,256,512]{2,1,0:T(8,128)}, u32[]{:S(2)}, u32[]{:S(2)}) collective-permute-start(f32[1,256,512]{2,1,0:T(8,128)} %get-tuple-element.1266), channel_id=1, source_target_pairs={{4,0},{5,1},{6,2},{7,3}} | collective-permute-start | bytes 1572872 | tf_op jit(solution)/shard_map/ppermute | solution.py:117
  516.7 3.5 copy-start.118
  516.7 3.5 copy-start.102
  547.0 6.1 copy-start.104
  562.1 3.2 copy-start.4
  598.2 5.1 copy-start.36
  598.2 5.1 copy-start.44
  603.3 3.3 copy-start.8
  618.4 12.9 %copy-start.13 = (bf16[4,8,256,256]{2,3,1,0:T(8,128)(2,1)}, bf16[4,8,256,256]{2,3,1,0:T(8,128)(2,1)S(1)}, u32[]{:S(2)}) copy-start(bf16[4,8,256,256]{2,3,1,0:T(8,128)(2,1)S(1)} %get-tuple-element.1146) | copy-start | bytes 12582916
  618.4 7.2 copy-start.42
  625.6 5.8 copy-start.52
  637.1 3.6 copy-start.90
  640.7 3.5 copy-start.120
  644.2 3.7 copy-start.37
  653.9 5.0 copy-start.16
  658.9 7.5 %copy-start.41 = (bf16[4,256,1,8,64]{1,4,3,0,2:T(8,128)(2,1)S(1)}, bf16[4,256,1,8,64]{1,4,3,0,2:T(8,128)(2,1)}, u32[]{:S(2)}) copy-start(bf16[4,256,1,8,64]{1,4,3,0,2:T(8,128)(2,1)} %copy.339) | copy-start | bytes 3145732
  658.9 15.5 %slice-start = ((s8[8388608]{0:T(1024)(128)(4,1)}), s8[4194304]{0:T(1024)(128)(4,1)S(1)}, s32[]{:S(2)}) async-start(s8[8388608]{0:T(1024)(128)(4,1)} %bitcast.1757), calls=%async_computation.2 | async-start | bytes 8388608
  666.4 8.0 %slice-start.1 = ((s8[8388608]{0:T(1024)(128)(4,1)}), s8[4194304]{0:T(1024)(128)(4,1)S(1)}, s32[]{:S(2)}) async-start(s8[8388608]{0:T(1024)(128)(4,1)} %bitcast.1757), calls=%async_computation.3 | async-start | bytes 8388608
  674.5 6.0 copy-start.3
  674.5 6.0 copy-start.17
  691.6 8.7 %copy-start.49 = (bf16[4,256,1,8,64]{1,4,3,0,2:T(8,128)(2,1)S(1)}, bf16[4,256,1,8,64]{1,4,3,0,2:T(8,128)(2,1)}, u32[]{:S(2)}) copy-start(bf16[4,256,1,8,64]{1,4,3,0,2:T(8,128)(2,1)} %copy.342) | copy-start | bytes 3145732
  (60 other events, 122.0 us)
Sparse Core Ops, SparseCore 0:
  161.7 160.8 all-gather.2
  572.7 20.6 all-gather.4
